TPU v7x, 128 devices: a whole 4x4x4 slice. The times are simulated.
128 devices in a mesh: row: 16 (over x, z), col: 8 (over y, core).
Axes of the slice: x: 4, y: 4, z: 4, core: 2. Of those that a mesh axis runs over, the one named last changes fastest.
Arguments:
- root_inverse: float32 [2, 2048, 4, 1024], P(None, 'row', None, 'col'), as said below
- child_coupling: float32 [2, 2, 2048, 2, 1024], P(None, None, 'row', None, 'col'), may hold values from -0.046875 to 0.046875
- child_inverse: float32 [2, 1, 2048, 2, 1024], P(None, None, 'row', None, 'col'), as said below
- pattern: int32 [2, 32], replicated, may hold values 0 or 1
Outputs:
- sigma_root: float32 [2, 2048, 4, 1024], P(None, 'row', None, 'col')
- sigma_coupling: float32 [2, 2, 2048, 2, 1024], P(None, None, 'row', None, 'col')
- sigma_child: float32 [2, 128, 2, 1024], P(None, None, None, 'col')
Inputs may be any that keep to these rules, and one draw needn't show every extreme that they name: `root_inverse`: read row-major as a 4096 x 4096 matrix it is lower triangular with a positive diagonal. `child_inverse`: read row-major each child's 2048 x 2048 matrix is lower triangular with a positive diagonal. `pattern`: 1 where child j's separator couples to root supernode i, else 0.
All inputs are finite; a program needn't handle non-finite values.
Results may differ from a plain program's by a relative error of at most 0.00013.
Values sent between devices are 32-bit elements; how exact they have to be, the bound alone decides.
No kernel may reach another device: no remote copies, remote signals or barrier semaphores. Data moves between devices by JAX's collectives and lax.ppermute only.
A program may use at most 128 MiB of HBM per device.

v0:
```python
import jax
import jax.numpy as jnp
from jax import lax
from jax.sharding import PartitionSpec as P

B = 128
NR = 4096
NC = 2048


def spread(value, axis, source):
    kept = jnp.where(lax.axis_index(axis) == source, value, 0).astype(value.dtype)
    return lax.psum(kept, axis)


def local(root_inverse, child_coupling, child_inverse, pattern):
    highest = lax.Precision.HIGHEST
    rows_axis = lax.axis_size("row")
    cols_axis = lax.axis_size("col")
    my_row = lax.axis_index("row")
    root_blocks, width, col_blocks, _ = root_inverse.shape
    child_count = child_coupling.shape[0]
    child_columns = child_coupling.shape[3]
    local_rows = root_blocks * width
    block_ids = jnp.arange(root_blocks, dtype=jnp.int32) * rows_axis + my_row
    matches = (jnp.arange(NR // B, dtype=jnp.int32)[None, :] == block_ids[:, None]).astype(
        jnp.float32
    )
    keep = jnp.einsum("jn,an->ja", pattern.astype(jnp.float32), matches)
    coupled = child_coupling * keep[:, :, None, None, None]
    root_panel, child_panel = (
        lax.all_gather(root_inverse, "row", axis=1, tiled=True),
        lax.all_gather(child_inverse, "row", axis=2, tiled=True),
    )
    columns = root_panel.reshape(NR, col_blocks * width)
    groups = rows_axis // cols_axis
    chosen = lax.dynamic_index_in_dim(
        columns.reshape(NR, root_blocks, groups, width), my_row // cols_axis, 2, False
    )
    mirrored = spread(chosen.reshape(NR, local_rows), "col", my_row % cols_axis)
    sigma_local = jnp.einsum("km,kn->mn", mirrored, columns, precision=highest)
    sigma_root = sigma_local.reshape(root_blocks, width, col_blocks, width)
    sigma_rows, coupling_rows = (
        lax.all_gather(sigma_root, "col", axis=3, tiled=True),
        lax.all_gather(coupled, "col", axis=4, tiled=True),
    )
    coupling_panel = coupling_rows.reshape(child_count, local_rows, NC)
    inverse_columns = child_panel.reshape(child_count, NC, child_columns * width)
    update = jnp.einsum("jmk,jkn->jmn", coupling_panel, inverse_columns, precision=highest)
    sigma_split = sigma_rows.reshape(local_rows, root_blocks, rows_axis * width)
    update_split = update.reshape(child_count, root_blocks, width, child_columns * width)
    product = jnp.einsum(
        "mak,jakn->jmn",
        sigma_split,
        lax.all_gather(update_split, "row", axis=2, tiled=True),
        precision=highest,
    )
    coupling_sigma = -(
        product.reshape(child_count, root_blocks, width, child_columns * width)
        * keep[:, :, None, None]
    )
    local_inverse = child_inverse.reshape(child_count, -1, child_columns, width)
    first_part = jnp.einsum("jkcr,jkcs->jcrs", local_inverse, local_inverse, precision=highest)
    update_blocks = update.reshape(child_count, local_rows, child_columns, width)
    sigma_blocks = coupling_sigma.reshape(child_count, local_rows, child_columns, width)
    second_part = jnp.einsum("jkcr,jkcs->jcrs", update_blocks, sigma_blocks, precision=highest)
    summed = lax.psum(first_part - second_part, "row")
    sigma_child = summed.transpose(0, 2, 1, 3)
    return (
        sigma_root,
        coupling_sigma.reshape(child_count, root_blocks, width, child_columns, width),
        sigma_child,
    )


def solution(mesh):
    in_specs = (
        P(None, "row", None, "col"),
        P(None, None, "row", None, "col"),
        P(None, None, "row", None, "col"),
        P(),
    )
    out_specs = (
        P(None, "row", None, "col"),
        P(None, None, "row", None, "col"),
        P(None, None, None, "col"),
    )
    return jax.shard_map(local, mesh=mesh, in_specs=in_specs, out_specs=out_specs, check_vma=False)
```

profile of v0, /device:TPU:0, one launch (start us, length us, event | category | flops | bytes accessed | tf_op | source)
XLA Modules:
  0.0 490.8 jit_solution(11845554919135694700)
XLA Ops:
  7.2 0.0 all-gather.6.cloned.1.call-start
  7.2 0.7 all-gather.6.cloned.1.call-update
  7.9 0.0 all-reduce.3.cloned.1.call-start
  8.0 75.6 %all-gather.6.cloned.1.call-done = f32[2,2048,4,128]{3,2,1,0:T(4,128)} async-done(((f32[2,128,4,128]{3,2,1,0:T(4,128)}), f32[2,2048,4,128]{3,2,1,0:T(4,128)}) %all-gather.6.cloned.1.call-update) | async-done | bytes 8388624 | tf_op jit(solution)/shard_map/all_gather | solution.py:32
  83.6 7.3 %broadcast_select_fusion = f32[4096,2,1,128]{3,2,1,0:T(1,128)} fusion(pred[]{:T(512)S(6)} %eq.18, f32[4096,2,2,128]{3,2,1,0:T(2,128)} %bitcast.53, s32[]{:T(128)S(6)} %select_n.29), kind=kLoop, calls=%fused_computation.1 | loop fusion | flops 1048576 | bytes 8388613 | tf_op jit(solution)/shard_map/jit(_where)/select_n | solution.py:12
  90.8 10.2 %copy.19 = f32[4096,2,1,128]{0,3,1,2:T(8,128)} copy(f32[4096,2,1,128]{3,2,1,0:T(1,128)} %broadcast_select_fusion) | data formatting | bytes 8388608 | tf_op jit(solution)/shard_map/jit(_where)/select_n | solution.py:12
  101.0 0.0 copy-start.3
  101.0 0.0 copy-start.2
  101.0 0.0 all-reduce.3.cloned.1.call-update
  101.0 0.0 all-gather.8.cloned.1.call-start
  101.1 0.6 copy-done.3
  101.7 0.2 convolution_bitcast_fusion
  101.9 0.1 copy.21
  102.0 0.1 copy-done.2
  102.1 1.0 broadcast_multiply_fusion
  103.1 0.0 all-gather.8.cloned.1.call-update
  103.1 0.0 all-gather.10.cloned.1.call-start
  103.2 0.5 all-gather.10.cloned.1.call-update
  103.7 0.0 all-gather.14.cloned.1.call-start
  103.7 7.6 %copy.44 = f32[512,8,4,128]{3,1,2,0:T(8,128)} copy(f32[512,8,4,128]{3,2,1,0:T(4,128)} %bitcast.54) | data formatting | bytes 16777216
  111.3 9.0 %copy.20 = f32[4096,512]{0,1:T(8,128)} copy(f32[4096,512]{1,0:T(8,128)} %bitcast.52) | data formatting | bytes 16777216 | tf_op jit(solution)/shard_map/reshape | solution.py:35
  120.3 53.0 %all-reduce.3.cloned.1.call-done = f32[2,128,4096]{2,1,0:T(8,128)} async-done(((f32[2,128,4096]{2,1,0:T(8,128)}), f32[2,128,4096]{2,1,0:T(8,128)}) %all-reduce.3.cloned.1.call-update) | async-done | bytes 4194320 | tf_op jit(solution)/shard_map/psum | solution.py:13
  173.3 11.0 %fusion = f32[2,128,4,128]{3,1,2,0:T(8,128)} fusion(f32[4,128,4096,1]{2,1,0,3:T(8,128)} %bitcast.51, f32[2,128,4096]{2,1,0:T(8,128)} %all-reduce.3.cloned.1.call-done), kind=kOutput, calls=%fused_computation.2 | convolution fusion | flops 6442450944 | bytes 13107200 | tf_op jit(solution)/shard_map/km,kn->mn/dot_general | solution.py:41
  184.3 0.0 all-gather.14.cloned.1.call-update
  184.3 0.0 all-gather.12.cloned.1.call-start
  184.4 27.3 %all-gather.8.cloned.1.call-done = f32[2,2,128,2,1024]{4,3,2,1,0:T(2,128)} async-done(((f32[2,2,128,2,128]{4,3,2,1,0:T(2,128)}), f32[2,2,128,2,1024]{4,3,2,1,0:T(2,128)}) %all-gather.8.cloned.1.call-update) | async-done | bytes 4194320 | tf_op jit(solution)/shard_map/all_gather | solution.py:45
  211.7 6.6 %reshape.53 = f32[2,256,2048]{2,1,0:T(8,128)} reshape(f32[2,2,128,2,1024]{4,3,2,1,0:T(2,128)} %all-gather.8.cloned.1.call-done) | data formatting | bytes 8388608 | tf_op jit(solution)/shard_map/reshape | solution.py:47
  218.3 48.1 %all-gather.10.cloned.1.call-done = f32[2,1,2048,2,128]{4,3,2,1,0:T(2,128)} async-done(((f32[2,1,128,2,128]{4,3,2,1,0:T(2,128)}), f32[2,1,2048,2,128]{4,3,2,1,0:T(2,128)}) %all-gather.10.cloned.1.call-update) | async-done | bytes 4194320 | tf_op jit(solution)/shard_map/all_gather | solution.py:33
  266.4 6.4 %reshape.54 = f32[2,2048,256]{2,1,0:T(8,128)} reshape(f32[2,1,2048,2,128]{4,3,2,1,0:T(2,128)} %all-gather.10.cloned.1.call-done) | data formatting | bytes 8388608 | tf_op jit(solution)/shard_map/reshape | solution.py:48
  272.9 8.1 %fusion.14 = f32[2,256,256]{2,1,0:T(8,128)S(1)} fusion(f32[2,256,2048]{2,1,0:T(8,128)} %reshape.53, f32[2,2048,256]{2,1,0:T(8,128)} %reshape.54), kind=kOutput, calls=%fused_computation.23 | convolution fusion | flops 3221225472 | bytes 8912896 | tf_op jit(solution)/shard_map/jmk,jkn->jmn/dot_general | solution.py:49
  280.9 1.0 copy.22
  281.9 0.0 all-gather.12.cloned.1.call-update
  282.0 0.2 all-reduce.5.cloned.1.call-start
  282.2 0.1 broadcast_bitcast_fusion
  282.3 0.2 copy.37
  282.5 21.7 %all-gather.14.cloned.1.call-done = f32[2,128,4,1024]{3,1,2,0:T(8,128)} async-done(((f32[2,128,4,128]{3,1,2,0:T(8,128)}), f32[2,128,4,1024]{3,1,2,0:T(8,128)}) %all-gather.14.cloned.1.call-update) | async-done | bytes 4194320 | tf_op jit(solution)/shard_map/all_gather | solution.py:44
  304.2 7.3 %copy.23 = f32[2,128,4,1024]{1,0,3,2:T(2,128)} copy(f32[2,128,4,1024]{3,1,2,0:T(8,128)} %all-gather.14.cloned.1.call-done) | data formatting | bytes 8388608 | tf_op jit(solution)/shard_map/all_gather | solution.py:44
  311.5 6.4 %reshape.56 = f32[256,2,2048]{0,2,1:T(8,128)} reshape(f32[2,128,4,1024]{1,0,3,2:T(2,128)} %copy.23) | data formatting | bytes 8388608 | tf_op jit(solution)/shard_map/reshape | solution.py:50
  317.9 0.0 copy-start.1
  317.9 0.0 copy-start
  317.9 68.3 %all-gather.12.cloned.1.call-done = f32[2,2,2048,256]{2,3,1,0:T(8,128)} async-done(((f32[2,2,128,256]{2,3,1,0:T(8,128)}), f32[2,2,2048,256]{2,3,1,0:T(8,128)}) %all-gather.12.cloned.1.call-update) | async-done | bytes 8388624 | tf_op jit(solution)/shard_map/all_gather | solution.py:55
  386.2 9.8 %fusion.2 = f32[2,256,256,1]{2,1,3,0:T(8,128)S(1)} fusion(f32[2,2,2048,256]{2,3,1,0:T(8,128)} %all-gather.12.cloned.1.call-done, f32[256,2,2048]{0,2,1:T(8,128)} %reshape.56), kind=kOutput, calls=%fused_computation.4 | convolution fusion | flops 6442450944 | bytes 13107200 | tf_op jit(solution)/shard_map/mak,jakn->jmn/dot_general | solution.py:52
  396.0 0.2 copy.29
  396.2 0.8 fusion.5
  397.0 0.0 copy-done.1
  397.0 1.3 fusion.4
  398.3 0.0 all-reduce.5.cloned.1.call-update
  398.3 0.0 copy-done
  398.3 1.1 copy.31
  399.5 0.3 reshape.57
  399.7 0.4 copy.25
  400.2 1.1 multiply_negate_fusion
  401.2 80.9 %all-reduce.5.cloned.1.call-done = f32[2,128,2,128]{3,1,2,0:T(8,128)} async-done(((f32[2,128,2,128]{3,1,2,0:T(8,128)}), f32[2,128,2,128]{3,1,2,0:T(8,128)}) %all-reduce.5.cloned.1.call-update) | async-done | bytes 262160 | tf_op jit(solution)/shard_map/psum | solution.py:67
  482.1 1.9 copy.32
  (2 shorter events, 0.0 us)
Async XLA Ops:
  7.2 76.4 %all-gather.6.cloned.1.call-start = ((), (), s32[]{:S(2)}) async-start(), calls=%async_computation | async-start | bytes 8912896 | tf_op jit(solution)/shard_map/all_gather | solution.py:32
  7.9 165.4 %all-reduce.3.cloned.1.call-start = ((), (), s32[]{:S(2)}) async-start(), calls=%async_computation.1 | async-start | bytes 8388608 | tf_op jit(solution)/shard_map/psum | solution.py:13
  101.0 0.7 copy-start.3
  101.0 1.1 copy-start.2
  101.0 110.6 %all-gather.8.cloned.1.call-start = ((), (), s32[]{:S(2)}) async-start(), calls=%async_computation.2 | async-start | bytes 4718592 | tf_op jit(solution)/shard_map/all_gather | solution.py:45
  103.1 163.3 %all-gather.10.cloned.1.call-start = ((), (), s32[]{:S(2)}) async-start(), calls=%async_computation.3 | async-start | bytes 4456448 | tf_op jit(solution)/shard_map/all_gather | solution.py:33
  103.7 200.5 %all-gather.14.cloned.1.call-start = ((), (), s32[]{:S(2)}) async-start(), calls=%async_computation.5 | async-start | bytes 4718592 | tf_op jit(solution)/shard_map/all_gather | solution.py:44
  184.3 201.9 %all-gather.12.cloned.1.call-start = ((), (), s32[]{:S(2)}) async-start(), calls=%async_computation.4 | async-start | bytes 8912896 | tf_op jit(solution)/shard_map/all_gather | solution.py:55
  282.0 200.1 %all-reduce.5.cloned.1.call-start = ((), (), s32[]{:S(2)}) async-start(), calls=%async_computation.6 | async-start | bytes 524288 | tf_op jit(solution)/shard_map/psum | solution.py:67
  317.9 79.1 %copy-start.1 = (f32[2,1,128,2,128]{4,3,2,1,0:T(2,128)S(1)}, f32[2,1,128,2,128]{4,3,2,1,0:T(2,128)}, u32[]{:S(2)}) copy-start(f32[2,1,128,2,128]{4,3,2,1,0:T(2,128)} %param.6) | copy-start | bytes 786436
  317.9 80.4 %copy-start = (f32[2,128,4,128]{3,1,2,0:T(8,128)S(1)}, f32[2,128,4,128]{3,1,2,0:T(8,128)}, u32[]{:S(2)}) copy-start(f32[2,128,4,128]{3,1,2,0:T(8,128)} %fusion) | copy-start | bytes 1572868
Sparse Core Ops, SparseCore 0:
  10.2 73.3 all-gather.5
  101.1 72.0 all-reduce.2
  175.5 36.0 all-gather.7
  213.7 52.6 all-gather.9
  268.5 35.6 all-gather.13
  306.7 79.4 all-gather.11
  398.4 83.6 all-reduce.4
where the time goes:
time: 492 us; the launch traced here: 491 us
  waiting for transfers between devices  376 us (76%)
  local copies, waits for them, and re-layouts  59.4 us (12%)
  matrix products  31.1 us (6%)
  between operations  14.2 us (3%)
  other arithmetic  9.37 us (2%)
    psum x1, waiting for transfers between devices, local(): summed = lax.psum(first_part - second_part, 'row')  80.9 us
    all_gather x1, waiting for transfers between devices, local(): lax.all_gather(root_inverse, 'row', axis=1, tiled=True)  75.6 us
    all_gather x1, waiting for transfers between devices, local(): lax.all_gather(update_split, 'row', axis=2, tiled=True)  68.3 us
    psum x1, waiting for transfers between devices, spread(): return lax.psum(kept, axis)  53 us
    all_gather x1, waiting for transfers between devices, local(): lax.all_gather(child_inverse, 'row', axis=2, tiled=True)  48.1 us
    all_gather x1, waiting for transfers between devices, local(): lax.all_gather(coupled, 'col', axis=4, tiled=True)  27.3 us
    all_gather x1, waiting for transfers between devices, local(): lax.all_gather(sigma_root, 'col', axis=3, tiled=True)  21.7 us
    unnamed x13, local copies, waits for them, and re-layouts  11.4 us
  transfers between devices with their start and end apart: 7, of which 7 were waited for; matrix products, arithmetic and copies ran while one was open for 14% of the time, Pallas kernels for 0%

commit v1 on v0

--- a/solution.py
+++ b/solution.py
@@ -6,6 +6,18 @@
 B = 128
 NR = 4096
 NC = 2048
+
+
+def product_in_turn(x, axis, dim, contribution):
+    size, index = (lax.axis_size(axis), lax.axis_index(axis))
+    left = [(i, (i - 1) % size) for i in range(size)]
+    span = x.shape[dim]
+    held = x
+    total = contribution(held, index * span)
+    for hop in range(1, size):
+        held = lax.ppermute(held, axis, left)
+        total = total + contribution(held, (index + hop) % size * span)
+    return total
 
 
 def spread(value, axis, source):
@@ -49,11 +61,16 @@
     update = jnp.einsum("jmk,jkn->jmn", coupling_panel, inverse_columns, precision=highest)
     sigma_split = sigma_rows.reshape(local_rows, root_blocks, rows_axis * width)
     update_split = update.reshape(child_count, root_blocks, width, child_columns * width)
-    product = jnp.einsum(
-        "mak,jakn->jmn",
-        sigma_split,
-        lax.all_gather(update_split, "row", axis=2, tiled=True),
-        precision=highest,
+    product = product_in_turn(
+        update_split,
+        "row",
+        2,
+        lambda part, start: jnp.einsum(
+            "mak,jakn->jmn",
+            lax.dynamic_slice_in_dim(sigma_split, start, part.shape[2], axis=2),
+            part,
+            precision=highest,
+        ),
     )
     coupling_sigma = -(
         product.reshape(child_count, root_blocks, width, child_columns * width)

time: 492 us -> 592 us (1.20)
  starting transfers between devices: 0.46 us -> 84.1 us
  matrix products: 31.1 us -> 38.2 us
    ppermute x0 -> x15, waiting for transfers between devices: none -> 120 us  [product_in_turn(): held = lax.ppermute(held, axis, left)]
    ppermute x0 -> x15, starting transfers between devices: none -> 83.9 us  [product_in_turn(): held = lax.ppermute(held, axis, left)]
    all_gather x1 -> x0, waiting for transfers between devices: 68.3 us -> none  [local(): lax.all_gather(update_split, 'row', axis=2, tiled=True)]
    all_gather x1, waiting for transfers between devices: 21.7 us -> 0.01 us  [local(): lax.all_gather(sigma_root, 'col', axis=3, tiled=True)]
    psum x1, waiting for transfers between devices: 53 us -> 40 us  [spread(): return lax.psum(kept, axis)]
    all_gather x1, waiting for transfers between devices: 27.3 us -> 20.3 us  [local(): lax.all_gather(coupled, 'col', axis=4, tiled=True)]
    dot_general x1 -> x16, matrix products: 9.78 us -> 16.2 us  [local(): jnp.einsum('mak,jakn->jmn', lax.dynamic_slice_in_dim(sigma_split, start,...]
    unnamed x13 -> x47, local copies, waits for them, and re-layouts: 11.4 us -> 16.6 us
  transfers between devices with their start and end apart: 7 -> 21, of which waited for: 7 -> 18; matrix products, arithmetic and copies ran while one was open for 14% -> 17% of each run, Pallas kernels for 0% -> 0%
where the time goes in v1:
time: 592 us; the launch traced here: 591 us
  waiting for transfers between devices  380 us (64%)
  starting transfers between devices  84.1 us (14%)
  local copies, waits for them, and re-layouts  64.1 us (11%)
  matrix products  38.2 us (6%)
  between operations  14.5 us (2%)
  other arithmetic  10.4 us (2%)
    ppermute x15, waiting for transfers between devices, product_in_turn(): held = lax.ppermute(held, axis, left)  120 us
    ppermute x15, starting transfers between devices, product_in_turn(): held = lax.ppermute(held, axis, left)  83.9 us
    psum x1, waiting for transfers between devices, local(): summed = lax.psum(first_part - second_part, 'row')  78 us
    all_gather x1, waiting for transfers between devices, local(): lax.all_gather(root_inverse, 'row', axis=1, tiled=True)  71.7 us
    all_gather x1, waiting for transfers between devices, local(): lax.all_gather(child_inverse, 'row', axis=2, tiled=True)  48.2 us
    psum x1, waiting for transfers between devices, spread(): return lax.psum(kept, axis)  40 us
    all_gather x1, waiting for transfers between devices, local(): lax.all_gather(coupled, 'col', axis=4, tiled=True)  20.3 us
    unnamed x47, local copies, waits for them, and re-layouts  16.6 us
  transfers between devices with their start and end apart: 21, of which 18 were waited for; matrix products, arithmetic and copies ran while one was open for 17% of the time, Pallas kernels for 0%

profile of v1, /device:TPU:0, one launch (start us, length us, event | category | flops | bytes accessed | tf_op | source)
XLA Modules:
  0.0 591.1 jit_solution(8841145771856567044)
XLA Ops:
  8.0 0.9 convolution_bitcast_fusion.16
  8.9 2.1 broadcast_multiply_fusion
  11.1 0.7 all-gather.9.cloned.1.call-update
  11.8 71.7 %all-gather.5.cloned.1.call-done = f32[2,2048,4,128]{3,2,1,0:T(4,128)} async-done(((f32[2,128,4,128]{3,2,1,0:T(4,128)}), f32[2,2048,4,128]{3,2,1,0:T(4,128)}) %all-gather.5.cloned.1.call-update) | async-done | bytes 8388624 | tf_op jit(solution)/shard_map/all_gather | solution.py:44
  83.6 7.3 %broadcast_select_fusion = f32[4096,2,1,128]{3,2,1,0:T(1,128)} fusion(pred[]{:T(512)S(6)} %eq.33, f32[4096,2,2,128]{3,2,1,0:T(2,128)} %bitcast.204, s32[]{:T(128)S(6)} %select_n.137), kind=kLoop, calls=%fused_computation.1 | loop fusion | flops 1048576 | bytes 8388613 | tf_op jit(solution)/shard_map/jit(_where)/select_n | solution.py:24
  90.8 10.3 %copy.20 = f32[4096,2,1,128]{0,3,1,2:T(8,128)} copy(f32[4096,2,1,128]{3,2,1,0:T(1,128)} %broadcast_select_fusion) | data formatting | bytes 8388608 | tf_op jit(solution)/shard_map/jit(_where)/select_n | solution.py:24
  101.2 20.3 %all-gather.7.cloned.1.call-done = f32[2,2,128,2,1024]{4,3,2,1,0:T(2,128)} async-done(((f32[2,2,128,2,128]{4,3,2,1,0:T(2,128)}), f32[2,2,128,2,1024]{4,3,2,1,0:T(2,128)}) %all-gather.7.cloned.1.call-update) | async-done | bytes 4194320 | tf_op jit(solution)/shard_map/all_gather | solution.py:57
  121.5 6.7 %reshape.53 = f32[2,256,2048]{2,1,0:T(8,128)} reshape(f32[2,2,128,2,1024]{4,3,2,1,0:T(2,128)} %all-gather.7.cloned.1.call-done) | data formatting | bytes 8388608 | tf_op jit(solution)/shard_map/reshape | solution.py:59
  128.2 48.2 %all-gather.9.cloned.1.call-done = f32[2,1,2048,2,128]{4,3,2,1,0:T(2,128)} async-done(((f32[2,1,128,2,128]{4,3,2,1,0:T(2,128)}), f32[2,1,2048,2,128]{4,3,2,1,0:T(2,128)}) %all-gather.9.cloned.1.call-update) | async-done | bytes 4194320 | tf_op jit(solution)/shard_map/all_gather | solution.py:45
  176.4 6.4 %reshape.54 = f32[2,2048,256]{2,1,0:T(8,128)} reshape(f32[2,1,2048,2,128]{4,3,2,1,0:T(2,128)} %all-gather.9.cloned.1.call-done) | data formatting | bytes 8388608 | tf_op jit(solution)/shard_map/reshape | solution.py:60
  182.8 8.1 %fusion.75 = f32[2,256,256]{2,1,0:T(8,128)S(1)} fusion(f32[2,256,2048]{2,1,0:T(8,128)} %reshape.53, f32[2,2048,256]{2,1,0:T(8,128)} %reshape.54), kind=kOutput, calls=%fused_computation.100 | convolution fusion | flops 3221225472 | bytes 8912896 | tf_op jit(solution)/shard_map/jmk,jkn->jmn/dot_general | solution.py:61
  191.1 3.0 collective-permute-start
  194.1 7.8 %copy.91 = f32[512,8,4,128]{3,1,2,0:T(8,128)} copy(f32[512,8,4,128]{3,2,1,0:T(4,128)} %bitcast.205) | data formatting | bytes 16777216
  201.9 9.1 %copy.21 = f32[4096,512]{0,1:T(8,128)} copy(f32[4096,512]{1,0:T(8,128)} %bitcast.203) | data formatting | bytes 16777216 | tf_op jit(solution)/shard_map/reshape | solution.py:47
  211.0 40.0 %all-reduce.3.cloned.1.call-done = f32[2,128,4096]{2,1,0:T(8,128)} async-done(((f32[2,128,4096]{2,1,0:T(8,128)}), f32[2,128,4096]{2,1,0:T(8,128)}) %all-reduce.3.cloned.1.call-update) | async-done | bytes 4194320 | tf_op jit(solution)/shard_map/psum | solution.py:25
  251.0 11.0 %fusion = f32[2,128,4,128]{3,1,2,0:T(8,128)} fusion(f32[4,128,4096,1]{2,1,0,3:T(8,128)} %bitcast.202, f32[2,128,4096]{2,1,0:T(8,128)} %all-reduce.3.cloned.1.call-done), kind=kOutput, calls=%fused_computation.2 | convolution fusion | flops 6442450944 | bytes 13107200 | tf_op jit(solution)/shard_map/km,kn->mn/dot_general | solution.py:53
  262.1 5.3 collective-permute-start.1
  267.4 9.4 %collective-permute-done.1 = f32[2,2,128,256]{2,3,1,0:T(8,128)S(1)} collective-permute-done((f32[2,2,128,256]{2,3,1,0:T(8,128)S(1)}, f32[2,2,128,256]{2,3,1,0:T(8,128)S(1)}, u32[]{:S(2)}, u32[]{:S(2)}) %collective-permute-start.1) | collective-permute-done | bytes 524320 | tf_op jit(solution)/shard_map/ppermute | solution.py:18
  276.9 5.8 collective-permute-start.2
  282.7 8.5 %collective-permute-done.2 = f32[2,2,128,256]{2,3,1,0:T(8,128)S(1)} collective-permute-done((f32[2,2,128,256]{2,3,1,0:T(8,128)S(1)}, f32[2,2,128,256]{2,3,1,0:T(8,128)S(1)}, u32[]{:S(2)}, u32[]{:S(2)}) %collective-permute-start.2) | collective-permute-done | bytes 524320 | tf_op jit(solution)/shard_map/ppermute | solution.py:18
  291.2 5.8 collective-permute-start.3
  297.0 7.6 %collective-permute-done.3 = f32[2,2,128,256]{2,3,1,0:T(8,128)S(1)} collective-permute-done((f32[2,2,128,256]{2,3,1,0:T(8,128)S(1)}, f32[2,2,128,256]{2,3,1,0:T(8,128)S(1)}, u32[]{:S(2)}, u32[]{:S(2)}) %collective-permute-start.3) | collective-permute-done | bytes 524320 | tf_op jit(solution)/shard_map/ppermute | solution.py:18
  304.6 5.8 collective-permute-start.4
  310.4 6.7 %collective-permute-done.4 = f32[2,2,128,256]{2,3,1,0:T(8,128)S(1)} collective-permute-done((f32[2,2,128,256]{2,3,1,0:T(8,128)S(1)}, f32[2,2,128,256]{2,3,1,0:T(8,128)S(1)}, u32[]{:S(2)}, u32[]{:S(2)}) %collective-permute-start.4) | collective-permute-done | bytes 524320 | tf_op jit(solution)/shard_map/ppermute | solution.py:18
  317.1 5.8 collective-permute-start.5
  322.9 6.9 %collective-permute-done.5 = f32[2,2,128,256]{2,3,1,0:T(8,128)S(1)} collective-permute-done((f32[2,2,128,256]{2,3,1,0:T(8,128)S(1)}, f32[2,2,128,256]{2,3,1,0:T(8,128)S(1)}, u32[]{:S(2)}, u32[]{:S(2)}) %collective-permute-start.5) | collective-permute-done | bytes 524320 | tf_op jit(solution)/shard_map/ppermute | solution.py:18
  329.8 0.8 copy-done.7
  330.6 5.8 collective-permute-start.6
  336.4 8.0 %collective-permute-done.6 = f32[2,2,128,256]{2,3,1,0:T(8,128)S(1)} collective-permute-done((f32[2,2,128,256]{2,3,1,0:T(8,128)S(1)}, f32[2,2,128,256]{2,3,1,0:T(8,128)S(1)}, u32[]{:S(2)}, u32[]{:S(2)}) %collective-permute-start.6) | collective-permute-done | bytes 524320 | tf_op jit(solution)/shard_map/ppermute | solution.py:18
  344.3 0.8 copy-done.9
  345.1 5.8 collective-permute-start.7
  351.0 9.1 %collective-permute-done.7 = f32[2,2,128,256]{2,3,1,0:T(8,128)S(1)} collective-permute-done((f32[2,2,128,256]{2,3,1,0:T(8,128)S(1)}, f32[2,2,128,256]{2,3,1,0:T(8,128)S(1)}, u32[]{:S(2)}, u32[]{:S(2)}) %collective-permute-start.7) | collective-permute-done | bytes 524320 | tf_op jit(solution)/shard_map/ppermute | solution.py:18
  360.0 0.8 copy-done.11
  360.8 5.8 collective-permute-start.8
  366.6 10.1 %collective-permute-done.8 = f32[2,2,128,256]{2,3,1,0:T(8,128)S(1)} collective-permute-done((f32[2,2,128,256]{2,3,1,0:T(8,128)S(1)}, f32[2,2,128,256]{2,3,1,0:T(8,128)S(1)}, u32[]{:S(2)}, u32[]{:S(2)}) %collective-permute-start.8) | collective-permute-done | bytes 524320 | tf_op jit(solution)/shard_map/ppermute | solution.py:18
  376.8 0.8 copy-done.13
  377.5 5.8 collective-permute-start.9
  383.3 11.3 %collective-permute-done.9 = f32[2,2,128,256]{2,3,1,0:T(8,128)S(1)} collective-permute-done((f32[2,2,128,256]{2,3,1,0:T(8,128)S(1)}, f32[2,2,128,256]{2,3,1,0:T(8,128)S(1)}, u32[]{:S(2)}, u32[]{:S(2)}) %collective-permute-start.9) | collective-permute-done | bytes 524320 | tf_op jit(solution)/shard_map/ppermute | solution.py:18
  394.6 0.8 copy-done.15
  395.4 5.8 collective-permute-start.10
  401.2 12.2 %collective-permute-done.10 = f32[2,2,128,256]{2,3,1,0:T(8,128)S(1)} collective-permute-done((f32[2,2,128,256]{2,3,1,0:T(8,128)S(1)}, f32[2,2,128,256]{2,3,1,0:T(8,128)S(1)}, u32[]{:S(2)}, u32[]{:S(2)}) %collective-permute-start.10) | collective-permute-done | bytes 524320 | tf_op jit(solution)/shard_map/ppermute | solution.py:18
  413.4 0.8 copy-done.17
  414.2 5.8 collective-permute-start.11
  420.0 11.4 %collective-permute-done.11 = f32[2,2,128,256]{2,3,1,0:T(8,128)S(1)} collective-permute-done((f32[2,2,128,256]{2,3,1,0:T(8,128)S(1)}, f32[2,2,128,256]{2,3,1,0:T(8,128)S(1)}, u32[]{:S(2)}, u32[]{:S(2)}) %collective-permute-start.11) | collective-permute-done | bytes 524320 | tf_op jit(solution)/shard_map/ppermute | solution.py:18
  431.4 0.8 copy-done.19
  432.3 5.8 collective-permute-start.12
  438.1 9.9 %collective-permute-done.12 = f32[2,2,128,256]{2,3,1,0:T(8,128)} collective-permute-done((f32[2,2,128,256]{2,3,1,0:T(8,128)S(1)}, f32[2,2,128,256]{2,3,1,0:T(8,128)}, u32[]{:S(2)}, u32[]{:S(2)}) %collective-permute-start.12) | collective-permute-done | bytes 524320 | tf_op jit(solution)/shard_map/ppermute | solution.py:18
  448.0 5.9 collective-permute-start.13
  454.2 9.0 %collective-permute-done.13 = f32[2,2,128,256]{2,3,1,0:T(8,128)} collective-permute-done((f32[2,2,128,256]{2,3,1,0:T(8,128)}, f32[2,2,128,256]{2,3,1,0:T(8,128)}, u32[]{:S(2)}, u32[]{:S(2)}) %collective-permute-start.13) | collective-permute-done | bytes 524320 | tf_op jit(solution)/shard_map/ppermute | solution.py:18
  463.2 5.8 collective-permute-start.14
  469.0 7.3 %copy.23 = f32[2,128,4,1024]{1,0,3,2:T(2,128)} copy(f32[2,128,4,1024]{3,1,2,0:T(8,128)} %all-gather.11.cloned.1.call-done) | data formatting | bytes 8388608 | tf_op jit(solution)/shard_map/all_gather | solution.py:56
  476.3 6.4 %reshape.56 = f32[256,2,2048]{0,2,1:T(8,128)} reshape(f32[2,128,4,1024]{1,0,3,2:T(2,128)} %copy.23) | data formatting | bytes 8388608 | tf_op jit(solution)/shard_map/reshape | solution.py:62
  482.7 2.1 convolution_bitcast_fusion.15
  484.8 1.6 fusion.2
  486.4 1.6 fusion.3
  494.2 1.7 fusion.14
  495.9 1.6 fusion.15
  497.6 1.6 fusion.16
  499.4 0.8 fusion.18
  500.2 1.3 fusion.17
  501.5 1.1 copy.48
  503.3 1.1 multiply_negate_fusion
  504.4 78.0 %all-reduce.5.cloned.1.call-done = f32[2,128,2,128]{3,1,2,0:T(8,128)} async-done(((f32[2,128,2,128]{3,1,2,0:T(8,128)}), f32[2,128,2,128]{3,1,2,0:T(8,128)}) %all-reduce.5.cloned.1.call-update) | async-done | bytes 262160 | tf_op jit(solution)/shard_map/psum | solution.py:84
  582.4 1.9 copy.49
  (68 shorter events, 8.4 us)
Async XLA Ops:
  7.2 76.4 %all-gather.5.cloned.1.call-start = ((), (), s32[]{:S(2)}) async-start(), calls=%async_computation | async-start | bytes 8912896 | tf_op jit(solution)/shard_map/all_gather | solution.py:44
  7.9 113.6 %all-gather.7.cloned.1.call-start = ((), (), s32[]{:S(2)}) async-start(), calls=%async_computation.2 | async-start | bytes 4718592 | tf_op jit(solution)/shard_map/all_gather | solution.py:57
  11.0 165.4 %all-gather.9.cloned.1.call-start = ((), (), s32[]{:S(2)}) async-start(), calls=%async_computation.3 | async-start | bytes 4456448 | tf_op jit(solution)/shard_map/all_gather | solution.py:45
  11.8 239.2 %all-reduce.3.cloned.1.call-start = ((), (), s32[]{:S(2)}) async-start(), calls=%async_computation.1 | async-start | bytes 8388608 | tf_op jit(solution)/shard_map/psum | solution.py:25
  101.1 367.9 %all-gather.11.cloned.1.call-start = ((), (), s32[]{:S(2)}) async-start(), calls=%async_computation.4 | async-start | bytes 4718592 | tf_op jit(solution)/shard_map/all_gather | solution.py:56
  191.1 71.0 %collective-permute-start = (f32[2,2,128,256]{2,3,1,0:T(8,128)S(1)}, f32[2,2,128,256]{2,3,1,0:T(8,128)S(1)}, u32[]{:S(2)}, u32[]{:S(2)}) collective-permute-start(f32[2,2,128,256]{2,3,1,0:T(8,128)S(1)} %copy.26), channel_id=1, source_target_pairs={{0,120},{8,0},{16,8},{24,16},{32,24},{40,32},{48,40},{56,48},{64,5... | collective-permute-start | bytes 1572872 | tf_op jit(solution)/shard_map/ppermute | solution.py:18
  262.0 320.4 %all-reduce.5.cloned.1.call-start = ((), (), s32[]{:S(2)}) async-start(), calls=%async_computation.5 | async-start | bytes 524288 | tf_op jit(solution)/shard_map/psum | solution.py:84
  262.1 14.8 %collective-permute-start.1 = (f32[2,2,128,256]{2,3,1,0:T(8,128)S(1)}, f32[2,2,128,256]{2,3,1,0:T(8,128)S(1)}, u32[]{:S(2)}, u32[]{:S(2)}) collective-permute-start(f32[2,2,128,256]{2,3,1,0:T(8,128)S(1)} %collective-permute-done), channel_id=1, source_target_pairs={{0,120},{8,0},{16,8},{24,16},{32,24},{40,32},{48,40},{56,48},{64,5... | collective-permute-start | bytes 1572872 | tf_op jit(solution)/shard_map/ppermute | solution.py:18
  276.9 14.3 %collective-permute-start.2 = (f32[2,2,128,256]{2,3,1,0:T(8,128)S(1)}, f32[2,2,128,256]{2,3,1,0:T(8,128)S(1)}, u32[]{:S(2)}, u32[]{:S(2)}) collective-permute-start(f32[2,2,128,256]{2,3,1,0:T(8,128)S(1)} %collective-permute-done.1), channel_id=1, source_target_pairs={{0,120},{8,0},{16,8},{24,16},{32,24},{40,32},{48,40},{56,48},{64,5... | collective-permute-start | bytes 1572872 | tf_op jit(solution)/shard_map/ppermute | solution.py:18
  291.2 13.4 %collective-permute-start.3 = (f32[2,2,128,256]{2,3,1,0:T(8,128)S(1)}, f32[2,2,128,256]{2,3,1,0:T(8,128)S(1)}, u32[]{:S(2)}, u32[]{:S(2)}) collective-permute-start(f32[2,2,128,256]{2,3,1,0:T(8,128)S(1)} %collective-permute-done.2), channel_id=1, source_target_pairs={{0,120},{8,0},{16,8},{24,16},{32,24},{40,32},{48,40},{56,48},{64,5... | collective-permute-start | bytes 1572872 | tf_op jit(solution)/shard_map/ppermute | solution.py:18
  304.6 171.7 %copy-start.3 = (f32[2,2,128,256]{2,3,1,0:T(8,128)}, f32[2,2,128,256]{2,3,1,0:T(8,128)S(1)}, u32[]{:S(2)}) copy-start(f32[2,2,128,256]{2,3,1,0:T(8,128)S(1)} %collective-permute-done.3) | copy-start | bytes 1572868
  304.6 12.5 %collective-permute-start.4 = (f32[2,2,128,256]{2,3,1,0:T(8,128)S(1)}, f32[2,2,128,256]{2,3,1,0:T(8,128)S(1)}, u32[]{:S(2)}, u32[]{:S(2)}) collective-permute-start(f32[2,2,128,256]{2,3,1,0:T(8,128)S(1)} %collective-permute-done.3), channel_id=1, source_target_pairs={{0,120},{8,0},{16,8},{24,16},{32,24},{40,32},{48,40},{56,48},{64,5... | collective-permute-start | bytes 1572872 | tf_op jit(solution)/shard_map/ppermute | solution.py:18
  317.1 136.9 %copy-start.5 = (f32[2,2,128,256]{2,3,1,0:T(8,128)}, f32[2,2,128,256]{2,3,1,0:T(8,128)S(1)}, u32[]{:S(2)}) copy-start(f32[2,2,128,256]{2,3,1,0:T(8,128)S(1)} %collective-permute-done.4) | copy-start | bytes 1572868
  317.1 12.7 %collective-permute-start.5 = (f32[2,2,128,256]{2,3,1,0:T(8,128)S(1)}, f32[2,2,128,256]{2,3,1,0:T(8,128)S(1)}, u32[]{:S(2)}, u32[]{:S(2)}) collective-permute-start(f32[2,2,128,256]{2,3,1,0:T(8,128)S(1)} %collective-permute-done.4), channel_id=1, source_target_pairs={{0,120},{8,0},{16,8},{24,16},{32,24},{40,32},{48,40},{56,48},{64,5... | collective-permute-start | bytes 1572872 | tf_op jit(solution)/shard_map/ppermute | solution.py:18
  329.8 0.8 copy-start.7
  330.6 13.8 %collective-permute-start.6 = (f32[2,2,128,256]{2,3,1,0:T(8,128)S(1)}, f32[2,2,128,256]{2,3,1,0:T(8,128)S(1)}, u32[]{:S(2)}, u32[]{:S(2)}) collective-permute-start(f32[2,2,128,256]{2,3,1,0:T(8,128)S(1)} %collective-permute-done.5), channel_id=1, source_target_pairs={{0,120},{8,0},{16,8},{24,16},{32,24},{40,32},{48,40},{56,48},{64,5... | collective-permute-start | bytes 1572872 | tf_op jit(solution)/shard_map/ppermute | solution.py:18
  344.3 0.8 copy-start.9
  345.1 14.9 %collective-permute-start.7 = (f32[2,2,128,256]{2,3,1,0:T(8,128)S(1)}, f32[2,2,128,256]{2,3,1,0:T(8,128)S(1)}, u32[]{:S(2)}, u32[]{:S(2)}) collective-permute-start(f32[2,2,128,256]{2,3,1,0:T(8,128)S(1)} %collective-permute-done.6), channel_id=1, source_target_pairs={{0,120},{8,0},{16,8},{24,16},{32,24},{40,32},{48,40},{56,48},{64,5... | collective-permute-start | bytes 1572872 | tf_op jit(solution)/shard_map/ppermute | solution.py:18
  360.0 0.8 copy-start.11
  360.8 15.9 %collective-permute-start.8 = (f32[2,2,128,256]{2,3,1,0:T(8,128)S(1)}, f32[2,2,128,256]{2,3,1,0:T(8,128)S(1)}, u32[]{:S(2)}, u32[]{:S(2)}) collective-permute-start(f32[2,2,128,256]{2,3,1,0:T(8,128)S(1)} %collective-permute-done.7), channel_id=1, source_target_pairs={{0,120},{8,0},{16,8},{24,16},{32,24},{40,32},{48,40},{56,48},{64,5... | collective-permute-start | bytes 1572872 | tf_op jit(solution)/shard_map/ppermute | solution.py:18
  376.8 0.8 copy-start.13
  377.5 17.1 %collective-permute-start.9 = (f32[2,2,128,256]{2,3,1,0:T(8,128)S(1)}, f32[2,2,128,256]{2,3,1,0:T(8,128)S(1)}, u32[]{:S(2)}, u32[]{:S(2)}) collective-permute-start(f32[2,2,128,256]{2,3,1,0:T(8,128)S(1)} %collective-permute-done.8), channel_id=1, source_target_pairs={{0,120},{8,0},{16,8},{24,16},{32,24},{40,32},{48,40},{56,48},{64,5... | collective-permute-start | bytes 1572872 | tf_op jit(solution)/shard_map/ppermute | solution.py:18
  394.6 0.8 copy-start.15
  395.4 18.0 %collective-permute-start.10 = (f32[2,2,128,256]{2,3,1,0:T(8,128)S(1)}, f32[2,2,128,256]{2,3,1,0:T(8,128)S(1)}, u32[]{:S(2)}, u32[]{:S(2)}) collective-permute-start(f32[2,2,128,256]{2,3,1,0:T(8,128)S(1)} %collective-permute-done.9), channel_id=1, source_target_pairs={{0,120},{8,0},{16,8},{24,16},{32,24},{40,32},{48,40},{56,48},{64,5... | collective-permute-start | bytes 1572872 | tf_op jit(solution)/shard_map/ppermute | solution.py:18
  413.4 0.8 copy-start.17
  414.2 17.2 %collective-permute-start.11 = (f32[2,2,128,256]{2,3,1,0:T(8,128)S(1)}, f32[2,2,128,256]{2,3,1,0:T(8,128)S(1)}, u32[]{:S(2)}, u32[]{:S(2)}) collective-permute-start(f32[2,2,128,256]{2,3,1,0:T(8,128)S(1)} %collective-permute-done.10), channel_id=1, source_target_pairs={{0,120},{8,0},{16,8},{24,16},{32,24},{40,32},{48,40},{56,48},{64,5... | collective-permute-start | bytes 1572872 | tf_op jit(solution)/shard_map/ppermute | solution.py:18
  431.4 0.8 copy-start.19
  432.3 15.7 %collective-permute-start.12 = (f32[2,2,128,256]{2,3,1,0:T(8,128)S(1)}, f32[2,2,128,256]{2,3,1,0:T(8,128)}, u32[]{:S(2)}, u32[]{:S(2)}) collective-permute-start(f32[2,2,128,256]{2,3,1,0:T(8,128)S(1)} %collective-permute-done.11), channel_id=1, source_target_pairs={{0,120},{8,0},{16,8},{24,16},{32,24},{40,32},{48,40},{56,48},{64,5... | collective-permute-start | bytes 1572872 | tf_op jit(solution)/shard_map/ppermute | solution.py:18
  448.0 15.2 %collective-permute-start.13 = (f32[2,2,128,256]{2,3,1,0:T(8,128)}, f32[2,2,128,256]{2,3,1,0:T(8,128)}, u32[]{:S(2)}, u32[]{:S(2)}) collective-permute-start(f32[2,2,128,256]{2,3,1,0:T(8,128)} %collective-permute-done.12), channel_id=1, source_target_pairs={{0,120},{8,0},{16,8},{24,16},{32,24},{40,32},{48,40},{56,48},{64,5... | collective-permute-start | bytes 1572872 | tf_op jit(solution)/shard_map/ppermute | solution.py:18
  463.2 34.4 %collective-permute-start.14 = (f32[2,2,128,256]{2,3,1,0:T(8,128)}, f32[2,2,128,256]{2,3,1,0:T(8,128)}, u32[]{:S(2)}, u32[]{:S(2)}) collective-permute-start(f32[2,2,128,256]{2,3,1,0:T(8,128)} %collective-permute-done.13), channel_id=1, source_target_pairs={{0,120},{8,0},{16,8},{24,16},{32,24},{40,32},{48,40},{56,48},{64,5... | collective-permute-start | bytes 1572872 | tf_op jit(solution)/shard_map/ppermute | solution.py:18
  482.7 5.3 copy-start
  482.7 6.0 %copy-start.4 = (f32[2,2,128,256]{2,3,1,0:T(8,128)S(1)}, f32[2,2,128,256]{2,3,1,0:T(8,128)}, u32[]{:S(2)}) copy-start(f32[2,2,128,256]{2,3,1,0:T(8,128)} %copy-done.3) | copy-start | bytes 1572868
  482.7 6.6 %copy-start.6 = (f32[2,2,128,256]{2,3,1,0:T(8,128)S(1)}, f32[2,2,128,256]{2,3,1,0:T(8,128)}, u32[]{:S(2)}) copy-start(f32[2,2,128,256]{2,3,1,0:T(8,128)} %copy-done.5) | copy-start | bytes 1572868
  484.8 5.1 copy-start.8
  486.4 4.1 copy-start.10
  488.1 3.1 copy-start.12
  488.7 3.1 copy-start.14
  489.3 3.1 copy-start.16
  489.9 3.1 copy-start.18
  490.5 3.0 copy-start.20
  494.2 6.0 %copy-start.2 = (f32[2,1,128,2,128]{4,3,2,1,0:T(2,128)S(1)}, f32[2,1,128,2,128]{4,3,2,1,0:T(2,128)}, u32[]{:S(2)}) copy-start(f32[2,1,128,2,128]{4,3,2,1,0:T(2,128)} %param.6) | copy-start | bytes 786436
  494.2 7.3 %copy-start.1 = (f32[2,128,4,128]{3,1,2,0:T(8,128)S(1)}, f32[2,128,4,128]{3,1,2,0:T(8,128)}, u32[]{:S(2)}) copy-start(f32[2,128,4,128]{3,1,2,0:T(8,128)} %fusion) | copy-start | bytes 1572868
Sparse Core Ops, SparseCore 0:
  10.2 73.3 all-gather.4
  85.8 35.6 all-gather.6
  123.7 52.6 all-gather.8
  178.6 72.3 all-reduce.2
  262.2 36.0 all-gather.10
  501.6 80.7 all-reduce.4
